TPU v7x, 256 devices: a whole 4x4x8 slice. The times are simulated.
256 devices in a mesh: loop: 4 (over y_hi, core), inner: 64 (over z, x, y_lo).
Axes of the slice: x: 4, y: 4 (y_hi: 2, y_lo: 2; y = y_hi * 2 + y_lo), z: 8, core: 2. Of those that a mesh axis runs over, the one named last changes fastest.
Arguments:
- snapshots: bfloat16 [65536, 1024], P(('loop', 'inner')), may hold values from -6 to 6
- bins: int32 [65536], replicated, may hold values from 0 to 511, as said below
- pairs: int32 [2048, 2], replicated, may hold values from 0 to 511, as said below
- start_weights: bfloat16 [1024, 32], replicated, may hold values from -0.1875 to 0.1875
Outputs:
- basis: float32 [65536, 96], P(('loop', 'inner'))
- coefficients: float32 [4, 32, 32], replicated
Inputs may be any that keep to these rules, and one draw needn't show every extreme that they name: `bins`: the snapshot in row n has a bin in [r * 8, (r + 1) * 8), where r = (n // 256) mod (64). `pairs`: every row (a, b) has a <= b <= a + 8; every bin is paired with itself.
All inputs are finite; a program needn't handle non-finite values.
Results may differ from a plain program's by a relative error of at most 0.0003.
Values may be sent and summed in bfloat16 or wider, within the bound.
A program may use at most 64 MiB of HBM per device.

v0:
```python
import jax
import jax.numpy as jnp
from jax import lax
from jax.sharding import PartitionSpec as P

STEPS = 2
BINS_COL = 8


def extended(cells, sides, width):
    for axis, dim in sides:
        count = lax.axis_size(axis)
        ends = count - 1
        head = lax.slice_in_dim(cells, 0, width, axis=dim)
        tail = lax.slice_in_dim(cells, cells.shape[dim] - width, cells.shape[dim], axis=dim)
        cells = jnp.concatenate(
            [
                lax.ppermute(tail, axis, [(i, (i + 1) % count) for i in range(ends)]),
                cells,
                lax.ppermute(head, axis, [((i + 1) % count, i) for i in range(ends)]),
            ],
            axis=dim,
        )
    return cells


def matches(values, targets):
    return (values[:, None] == targets[None, :]).astype(jnp.float32)


def local_gram(left, right):
    return jnp.dot(left.T, right, precision=lax.Precision.HIGHEST)


def finish(matrix, gram_total):
    lower_factor = jnp.linalg.cholesky(gram_total)
    result = lax.linalg.triangular_solve(
        lower_factor, matrix, left_side=False, lower=True, transpose_a=True
    )
    return (result, lower_factor.T)


def local(snapshots, bins, pairs, start_weights):
    row_count, features = snapshots.shape
    block_width = start_weights.shape[1]
    n_loop = lax.axis_size("loop")
    n_inner = lax.axis_size("inner")
    column = lax.axis_index("inner")
    group = lax.axis_index("loop")
    bin_grid = jnp.pad(
        bins.reshape(n_loop, n_inner, row_count), ((0, 0), (1, 1), (0, 0)), constant_values=-1
    )
    stacked = lax.all_gather(snapshots[None], "loop", axis=0, tiled=True)
    partner_rows = extended(stacked, (("inner", 1),), row_count)
    tile_rows = partner_rows.reshape(n_loop * 3 * row_count, features)
    tile_bins = lax.dynamic_slice_in_dim(bin_grid, column, 3, 1).reshape(-1)
    my_bins = lax.dynamic_slice_in_dim(bins, (group * n_inner + column) * row_count, row_count)
    bin_base = column * BINS_COL
    my_ids = bin_base + jnp.arange(BINS_COL, dtype=jnp.int32)
    window_ids = bin_base - BINS_COL + jnp.arange(3 * BINS_COL, dtype=jnp.int32)
    left_bins = pairs[:, 0]
    right_bins = pairs[:, 1]
    pair_count = jnp.dot(
        matches(left_bins, my_ids).T,
        matches(right_bins, window_ids),
        precision=lax.Precision.HIGHEST,
    )
    pair_count = pair_count + jnp.dot(
        matches(right_bins, my_ids).T,
        matches(left_bins, window_ids),
        precision=lax.Precision.HIGHEST,
    )
    linked_bins = jnp.where(pair_count > 0.5, 1.0, 0.0).astype(jnp.float32)
    my_hot = matches(my_bins, my_ids)
    row_links = jnp.dot(my_hot, linked_bins)
    mine_wide = snapshots.astype(jnp.float32)
    mine_norms = jnp.sum(mine_wide * mine_wide, axis=1)
    epsilon = features / 3.0
    part_hot = matches(tile_bins, window_ids) * (tile_bins >= 0).astype(jnp.float32)[:, None]
    band_mask = jnp.dot(row_links, part_hot.T)
    part_wide = tile_rows.astype(jnp.float32)
    part_norms = jnp.sum(part_wide * part_wide, axis=1)
    products = lax.dot_general(
        snapshots, tile_rows, (((1,), (1,)), ((), ())), preferred_element_type=jnp.float32
    )
    distance = mine_norms[:, None] + part_norms[None, :] - 2.0 * products
    kept_tiles = [band_mask * jnp.exp(-distance / epsilon)]

    def current_kernel(which):
        return kept_tiles[which]

    degree = jnp.sum(current_kernel(0), axis=1)
    inv_root = lax.rsqrt(degree)
    start_block = jnp.dot(snapshots, start_weights, preferred_element_type=jnp.float32)
    start_total = lax.psum(local_gram(start_block, start_block), ("loop", "inner"))
    current, unused = finish(start_block, start_total)
    basis_blocks = [current]
    coefficients = []
    previous = current
    prev_b = jnp.zeros((block_width, block_width), jnp.float32)
    for lanczos_step in range(STEPS):
        scaled = inv_root[:, None] * current
        vec_stack = lax.all_gather(scaled[None], "loop", axis=0, tiled=True)
        vec_strip = extended(vec_stack, (("inner", 1),), row_count)
        strip = vec_strip.reshape(n_loop * 3 * row_count, block_width)
        total = jnp.dot(current_kernel(0), strip, precision=lax.Precision.HIGHEST)
        image = inv_root[:, None] * total
        projected = lax.psum(local_gram(current, image), ("loop", "inner"))
        image = image - jnp.dot(current, projected, precision=lax.Precision.HIGHEST)
        if lanczos_step > 0:
            image = image - jnp.dot(previous, prev_b.T, precision=lax.Precision.HIGHEST)
        gram_total = lax.psum(local_gram(image, image), ("loop", "inner"))
        following, factor = finish(image, gram_total)
        coefficients.append(projected)
        coefficients.append(factor)
        previous = current
        prev_b = factor
        current = following
        basis_blocks.append(current)
    return (jnp.concatenate(basis_blocks, axis=1), jnp.stack(coefficients))


def solution(mesh):
    in_specs = (P(("loop", "inner"), None), P(), P(), P())
    out_specs = (P(("loop", "inner"), None), P())
    return jax.shard_map(local, mesh=mesh, in_specs=in_specs, out_specs=out_specs, check_vma=False)
```

profile of v0, /device:TPU:1, one launch (start us, length us, event | category | flops | bytes accessed | tf_op | source)
XLA Modules:
  0.0 579.3 jit_solution(10393950573843033094)
XLA Ops:
  11.2 90.2 %psum.35 = f32[32,32]{0,1:T(8,128)S(1)} all-reduce(f32[32,32]{0,1:T(8,128)S(1)} %fusion.50), channel_id=1, replica_groups=mesh['loop'=4,'inner'=64] {'loop','inner'}, use_global_device_ids=true, to_apply=%region_0.1 | all-reduce | flops 1024 | bytes 8192 | tf_op jit(solution)/shard_map/psum | solution.py:95
  102.8 5.3 collective-permute-start
  108.1 2.9 cholesky.59
  112.4 2.4 custom-call.7
  118.8 31.0 %collective-permute-done.1 = bf16[4,256,1024]{2,1,0:T(8,128)(2,1)S(1)} collective-permute-done((bf16[4,256,1024]{2,1,0:T(8,128)(2,1)}, bf16[4,256,1024]{2,1,0:T(8,128)(2,1)S(1)}, u32[]{:S(2)}, u32[]{:S(2)}) %collective-permute-start.1) | collective-permute-done | bytes 2097184 | tf_op jit(solution)/shard_map/ppermute | solution.py:20
  149.8 44.7 %collective-permute-done = bf16[4,256,1024]{2,1,0:T(8,128)(2,1)} collective-permute-done((bf16[4,256,1024]{2,1,0:T(8,128)(2,1)}, bf16[4,256,1024]{2,1,0:T(8,128)(2,1)}, u32[]{:S(2)}, u32[]{:S(2)}) %collective-permute-start) | collective-permute-done | bytes 2097184 | tf_op jit(solution)/shard_map/ppermute | solution.py:18
  194.5 3.6 multiply_reduce_fusion
  198.2 3.5 fusion
  201.7 3.1 fusion.46
  205.0 7.2 %all-gather.1 = f32[1024,32]{0,1:T(8,128)S(1)} all-gather(f32[256,32]{0,1:T(8,128)S(1)} %get-tuple-element.20), channel_id=3, replica_groups=mesh['loop'=4,'inner'=64] {'loop'}, dimensions={0}, use_global_device_ids=true | all-gather | bytes 163840 | tf_op jit(solution)/shard_map/all_gather | solution.py:103
  213.6 4.8 collective-permute-start.2
  220.2 3.2 collective-permute-done.2
  223.6 2.8 convolution_multiply_fusion.3
  226.5 80.3 %psum.36 = f32[32,32]{0,1:T(8,128)S(1)} all-reduce(f32[32,32]{0,1:T(8,128)S(1)} %fusion.51), channel_id=1, replica_groups=mesh['loop'=4,'inner'=64] {'loop','inner'}, use_global_device_ids=true, to_apply=%region_6.9 | all-reduce | flops 1024 | bytes 8192 | tf_op jit(solution)/shard_map/psum | solution.py:108
  307.2 75.5 %psum.37 = f32[32,32]{0,1:T(8,128)S(1)} all-reduce(f32[32,32]{0,1:T(8,128)S(1)} %fusion.52), channel_id=1, replica_groups=mesh['loop'=4,'inner'=64] {'loop','inner'}, use_global_device_ids=true, to_apply=%region_7.10 | all-reduce | flops 1024 | bytes 8192 | tf_op jit(solution)/shard_map/psum | solution.py:112
  382.8 2.9 cholesky.70
  390.3 7.4 %all-gather.2 = f32[1024,32]{0,1:T(8,128)S(1)} all-gather(f32[256,32]{0,1:T(8,128)S(1)} %get-tuple-element.22), channel_id=4, replica_groups=mesh['loop'=4,'inner'=64] {'loop'}, dimensions={0}, use_global_device_ids=true | all-gather | bytes 163840 | tf_op jit(solution)/shard_map/all_gather | solution.py:103
  399.1 4.0 collective-permute-start.4
  404.7 2.6 collective-permute-done.4
  407.5 3.5 convolution_multiply_fusion.2
  411.1 76.5 %psum.38 = f32[32,32]{0,1:T(8,128)S(1)} all-reduce(f32[32,32]{0,1:T(8,128)S(1)} %fusion.53), channel_id=1, replica_groups=mesh['loop'=4,'inner'=64] {'loop','inner'}, use_global_device_ids=true, to_apply=%region_8.11 | all-reduce | flops 1024 | bytes 8192 | tf_op jit(solution)/shard_map/psum | solution.py:108
  488.7 75.3 %psum.39 = f32[32,32]{0,1:T(8,128)S(1)} all-reduce(f32[32,32]{0,1:T(8,128)S(1)} %fusion.54), channel_id=1, replica_groups=mesh['loop'=4,'inner'=64] {'loop','inner'}, use_global_device_ids=true, to_apply=%region_9.12 | all-reduce | flops 1024 | bytes 8192 | tf_op jit(solution)/shard_map/psum | solution.py:112
  564.1 2.9 cholesky.81
  568.4 2.4 custom-call.9
  (70 shorter events, 26.8 us)
Async XLA Ops:
  7.2 2.6 copy-start
  7.2 94.4 %all-gather.5.cloned.1.call-start = ((), (), s32[]{:S(2)}) async-start(), calls=%async_computation | async-start | bytes 2621440 | tf_op jit(solution)/shard_map/all_gather | solution.py:53
  101.5 48.3 %collective-permute-start.1 = (bf16[4,256,1024]{2,1,0:T(8,128)(2,1)}, bf16[4,256,1024]{2,1,0:T(8,128)(2,1)S(1)}, u32[]{:S(2)}, u32[]{:S(2)}) collective-permute-start(bf16[4,256,1024]{2,1,0:T(8,128)(2,1)} %bitcast.93), channel_id=1, source_target_pairs={{1,0},{2,1},{3,2},{4,3},{5,4},{6,5},{7,6},{8,7},{9,8},{10,9},{11,1... | collective-permute-start | bytes 6291464 | tf_op jit(solution)/shard_map/ppermute | solution.py:20
  102.8 91.7 %collective-permute-start = (bf16[4,256,1024]{2,1,0:T(8,128)(2,1)}, bf16[4,256,1024]{2,1,0:T(8,128)(2,1)}, u32[]{:S(2)}, u32[]{:S(2)}) collective-permute-start(bf16[4,256,1024]{2,1,0:T(8,128)(2,1)} %bitcast.94), channel_id=1, source_target_pairs={{0,1},{1,2},{2,3},{3,4},{4,5},{5,6},{6,7},{7,8},{8,9},{9,10},{10,1... | collective-permute-start | bytes 6291464 | tf_op jit(solution)/shard_map/ppermute | solution.py:18
  118.8 79.3 %copy-start.1 = (bf16[256,1024]{1,0:T(8,128)(2,1)S(1)}, bf16[256,1024]{1,0:T(8,128)(2,1)}, u32[]{:S(2)}) copy-start(bf16[256,1024]{1,0:T(8,128)(2,1)} %param.7) | copy-start | bytes 1572868
  204.8 185.5 %copy-start.5 = (f32[256]{0:T(256)}, f32[256]{0:T(256)S(1)}, u32[]{:S(2)}) copy-start(f32[256]{0:T(256)S(1)} %rsqrt.7) | copy-start | bytes 3076
  212.3 7.9 %collective-permute-start.3 = (f32[4,256,32]{1,0,2:T(4,128)S(1)}, f32[4,256,32]{1,0,2:T(4,128)S(1)}, u32[]{:S(2)}, u32[]{:S(2)}) collective-permute-start(f32[4,256,32]{1,0,2:T(4,128)S(1)} %reshape.60), channel_id=1, source_target_pairs={{1,0},{2,1},{3,2},{4,3},{5,4},{6,5},{7,6},{8,7},{9,8},{10,9},{11,1... | collective-permute-start | bytes 393224 | tf_op jit(solution)/shard_map/ppermute | solution.py:20
  213.6 9.8 %collective-permute-start.2 = (f32[4,256,32]{1,0,2:T(4,128)S(1)}, f32[4,256,32]{1,0,2:T(4,128)S(1)}, u32[]{:S(2)}, u32[]{:S(2)}) collective-permute-start(f32[4,256,32]{1,0,2:T(4,128)S(1)} %reshape.60), channel_id=1, source_target_pairs={{0,1},{1,2},{2,3},{3,4},{4,5},{5,6},{6,7},{7,8},{8,9},{9,10},{10,1... | collective-permute-start | bytes 393224 | tf_op jit(solution)/shard_map/ppermute | solution.py:18
  306.9 83.4 %copy-start.2 = (f32[32,32]{0,1:T(8,128)}, f32[32,32]{0,1:T(8,128)S(1)}, u32[]{:S(2)}) copy-start(f32[32,32]{0,1:T(8,128)S(1)} %psum.36) | copy-start | bytes 12292
  397.8 173.9 %copy-start.3 = (f32[32,32]{0,1:T(8,128)S(1)}, f32[32,32]{0,1:T(8,128)}, u32[]{:S(2)}) copy-start(f32[32,32]{0,1:T(8,128)} %copy-done.2) | copy-start | bytes 12292
  397.8 173.9 %copy-start.4 = (f32[1,32,32]{1,2,0:T(8,128)S(1)}, f32[1,32,32]{1,2,0:T(8,128)}, u32[]{:S(2)}) copy-start(f32[1,32,32]{1,2,0:T(8,128)} %get-tuple-element.12) | copy-start | bytes 12292
  397.8 6.8 %collective-permute-start.5 = (f32[4,256,32]{1,0,2:T(4,128)S(1)}, f32[4,256,32]{1,0,2:T(4,128)S(1)}, u32[]{:S(2)}, u32[]{:S(2)}) collective-permute-start(f32[4,256,32]{1,0,2:T(4,128)S(1)} %reshape.61), channel_id=1, source_target_pairs={{1,0},{2,1},{3,2},{4,3},{5,4},{6,5},{7,6},{8,7},{9,8},{10,9},{11,1... | collective-permute-start | bytes 393224 | tf_op jit(solution)/shard_map/ppermute | solution.py:20
  399.1 8.2 %collective-permute-start.4 = (f32[4,256,32]{1,0,2:T(4,128)S(1)}, f32[4,256,32]{1,0,2:T(4,128)S(1)}, u32[]{:S(2)}, u32[]{:S(2)}) collective-permute-start(f32[4,256,32]{1,0,2:T(4,128)S(1)} %reshape.61), channel_id=1, source_target_pairs={{0,1},{1,2},{2,3},{3,4},{4,5},{5,6},{6,7},{7,8},{8,9},{9,10},{10,1... | collective-permute-start | bytes 393224 | tf_op jit(solution)/shard_map/ppermute | solution.py:18
Sparse Core Ops, SparseCore 0:
  9.8 33.8 all-gather.4
where the time goes:
time: 581 us; the launch traced here: 579 us
  blocking collectives  413 us (71%)
  waiting for transfers between devices  85.5 us (15%)
  other arithmetic  26.3 us (5%)
  matrix products  18.7 us (3%)
  starting transfers between devices  17.9 us (3%)
  between operations  14.3 us (2%)
    psum x2, blocking collectives, local(): projected = lax.psum(local_gram(current, image), ('loop', 'inner'))  157 us
    psum x2, blocking collectives, local(): gram_total = lax.psum(local_gram(image, image), ('loop', 'inner'))  151 us
    psum x1, blocking collectives, local(): lax.psum(local_gram(start_block, start_block), ('loop', 'inner'))  90.2 us
    ppermute x3, waiting for transfers between devices, extended(): lax.ppermute(tail, axis, [(i, (i + 1) % count) for i in range(ends)])  50.5 us
    ppermute x3, waiting for transfers between devices, extended(): lax.ppermute(head, axis, [((i + 1) % count, i) for i in range(ends)])  34.4 us
    all_gather x2, blocking collectives, local(): vec_stack = lax.all_gather(scaled[None], 'loop', axis=0, tiled=True)  14.7 us
    ppermute x3, starting transfers between devices, extended(): lax.ppermute(tail, axis, [(i, (i + 1) % count) for i in range(ends)])  14 us
  transfers between devices with their start and end apart: 7, of which 6 were waited for; matrix products, arithmetic and copies ran while one was open for 2% of the time, Pallas kernels for 0%

commit v1 on v0

--- a/solution.py
+++ b/solution.py
@@ -109,7 +109,8 @@
         image = image - jnp.dot(current, projected, precision=lax.Precision.HIGHEST)
         if lanczos_step > 0:
             image = image - jnp.dot(previous, prev_b.T, precision=lax.Precision.HIGHEST)
-        gram_total = lax.psum(local_gram(image, image), ("loop", "inner"))
+        one_axis = lax.psum(local_gram(image, image), "inner")
+        gram_total = lax.psum(one_axis, "loop")
         following, factor = finish(image, gram_total)
         coefficients.append(projected)
         coefficients.append(factor)

time: 581 us -> 1070 us (1.84)
  blocking collectives: 413 us -> 900 us
    psum x2 -> x4, blocking collectives: 151 us -> 636 us  [the longest x2 503 us: local(): one_axis = lax.psum(local_gram(image, image), 'inner')]
  transfers between devices with their start and end apart: 7 -> 7, of which waited for: 6 -> 6; matrix products, arithmetic and copies ran while one was open for 2% -> 1% of each run, Pallas kernels for 0% -> 0%
where the time goes in v1:
time: 1070 us
  blocking collectives  900 us (84%)
  waiting for transfers between devices  83.8 us (8%)
  other arithmetic  26.3 us (2%)
  matrix products  18.7 us (2%)
  starting transfers between devices  17.9 us (2%)
  between operations  14.3 us (1%)
    psum x2, blocking collectives, local(): one_axis = lax.psum(local_gram(image, image), 'inner')  503 us
    psum x2, blocking collectives, local(): projected = lax.psum(local_gram(current, image), ('loop', 'inner'))  157 us
    psum x2, blocking collectives, local(): gram_total = lax.psum(one_axis, 'loop')  133 us
    psum x1, blocking collectives, local(): lax.psum(local_gram(start_block, start_block), ('loop', 'inner'))  90.2 us
    ppermute x3, waiting for transfers between devices, extended(): lax.ppermute(tail, axis, [(i, (i + 1) % count) for i in range(ends)])  48.7 us
    ppermute x3, waiting for transfers between devices, extended(): lax.ppermute(head, axis, [((i + 1) % count, i) for i in range(ends)])  34.4 us
  transfers between devices with their start and end apart: 7, of which 6 were waited for; matrix products, arithmetic and copies ran while one was open for 1% of the time, Pallas kernels for 0%

profile of v1, /device:TPU:1, one launch (start us, length us, event | category | flops | bytes accessed | tf_op | source)
XLA Modules:
  0.0 1065.1 jit_solution(4597895202075452865)
XLA Ops:
  11.2 90.2 %psum.49 = f32[32,32]{0,1:T(8,128)S(1)} all-reduce(f32[32,32]{0,1:T(8,128)S(1)} %fusion.50), channel_id=1, replica_groups=mesh['loop'=4,'inner'=64] {'loop','inner'}, use_global_device_ids=true, to_apply=%region_0.1 | all-reduce | flops 1024 | bytes 8192 | tf_op jit(solution)/shard_map/psum | solution.py:95
  102.8 5.3 collective-permute-start
  108.1 2.9 cholesky.59
  112.4 2.4 custom-call.7
  118.8 31.0 %collective-permute-done.1 = bf16[4,256,1024]{2,1,0:T(8,128)(2,1)S(1)} collective-permute-done((bf16[4,256,1024]{2,1,0:T(8,128)(2,1)}, bf16[4,256,1024]{2,1,0:T(8,128)(2,1)S(1)}, u32[]{:S(2)}, u32[]{:S(2)}) %collective-permute-start.1) | collective-permute-done | bytes 2097184 | tf_op jit(solution)/shard_map/ppermute | solution.py:20
  149.8 44.7 %collective-permute-done = bf16[4,256,1024]{2,1,0:T(8,128)(2,1)} collective-permute-done((bf16[4,256,1024]{2,1,0:T(8,128)(2,1)}, bf16[4,256,1024]{2,1,0:T(8,128)(2,1)}, u32[]{:S(2)}, u32[]{:S(2)}) %collective-permute-start) | collective-permute-done | bytes 2097184 | tf_op jit(solution)/shard_map/ppermute | solution.py:18
  194.5 3.6 multiply_reduce_fusion
  198.2 3.5 fusion
  201.7 3.1 fusion.46
  205.0 7.2 all-gather.1
  213.6 4.8 collective-permute-start.2
  220.2 3.2 collective-permute-done.2
  223.6 2.8 convolution_multiply_fusion.3
  226.5 80.3 %psum.50 = f32[32,32]{0,1:T(8,128)S(1)} all-reduce(f32[32,32]{0,1:T(8,128)S(1)} %fusion.51), channel_id=1, replica_groups=mesh['loop'=4,'inner'=64] {'loop','inner'}, use_global_device_ids=true, to_apply=%region_6.9 | all-reduce | flops 1024 | bytes 8192 | tf_op jit(solution)/shard_map/psum | solution.py:108
  307.2 251.4 %psum.51 = f32[32,32]{0,1:T(8,128)S(1)} all-reduce(f32[32,32]{0,1:T(8,128)S(1)} %fusion.52), channel_id=1, replica_groups=mesh['loop'=4,'inner'=64] {'inner'}, use_global_device_ids=true, to_apply=%region_7.10 | all-reduce | flops 1024 | bytes 8192 | tf_op jit(solution)/shard_map/psum | solution.py:112
  558.6 66.7 %psum.52 = f32[32,32]{0,1:T(8,128)S(1)} all-reduce(f32[32,32]{0,1:T(8,128)S(1)} %psum.51), channel_id=1, replica_groups=mesh['loop'=4,'inner'=64] {'loop'}, use_global_device_ids=true, to_apply=%region_8.11 | all-reduce | flops 1024 | bytes 8192 | tf_op jit(solution)/shard_map/psum | solution.py:113
  625.3 2.9 cholesky.70
  632.8 9.5 all-gather.2
  643.7 4.0 collective-permute-start.4
  650.3 3.5 convolution_multiply_fusion.2
  653.9 76.9 %psum.53 = f32[32,32]{0,1:T(8,128)S(1)} all-reduce(f32[32,32]{0,1:T(8,128)S(1)} %fusion.53), channel_id=1, replica_groups=mesh['loop'=4,'inner'=64] {'loop','inner'}, use_global_device_ids=true, to_apply=%region_9.12 | all-reduce | flops 1024 | bytes 8192 | tf_op jit(solution)/shard_map/psum | solution.py:108
  731.9 251.4 %psum.54 = f32[32,32]{0,1:T(8,128)S(1)} all-reduce(f32[32,32]{0,1:T(8,128)S(1)} %fusion.54), channel_id=1, replica_groups=mesh['loop'=4,'inner'=64] {'inner'}, use_global_device_ids=true, to_apply=%region_10.13 | all-reduce | flops 1024 | bytes 8192 | tf_op jit(solution)/shard_map/psum | solution.py:112
  983.3 66.5 %psum.55 = f32[32,32]{0,1:T(8,128)S(1)} all-reduce(f32[32,32]{0,1:T(8,128)S(1)} %psum.54), channel_id=1, replica_groups=mesh['loop'=4,'inner'=64] {'loop'}, use_global_device_ids=true, to_apply=%region_11.14 | all-reduce | flops 1024 | bytes 8192 | tf_op jit(solution)/shard_map/psum | solution.py:113
  1049.9 2.9 cholesky.81
  (72 shorter events, 30.1 us)
Async XLA Ops:
  7.2 2.6 copy-start
  7.2 94.4 %all-gather.5.cloned.1.call-start = ((), (), s32[]{:S(2)}) async-start(), calls=%async_computation | async-start | bytes 2621440 | tf_op jit(solution)/shard_map/all_gather | solution.py:53
  101.5 48.3 %collective-permute-start.1 = (bf16[4,256,1024]{2,1,0:T(8,128)(2,1)}, bf16[4,256,1024]{2,1,0:T(8,128)(2,1)S(1)}, u32[]{:S(2)}, u32[]{:S(2)}) collective-permute-start(bf16[4,256,1024]{2,1,0:T(8,128)(2,1)} %bitcast.93), channel_id=1, source_target_pairs={{1,0},{2,1},{3,2},{4,3},{5,4},{6,5},{7,6},{8,7},{9,8},{10,9},{11,1... | collective-permute-start | bytes 6291464 | tf_op jit(solution)/shard_map/ppermute | solution.py:20
  102.8 91.7 %collective-permute-start = (bf16[4,256,1024]{2,1,0:T(8,128)(2,1)}, bf16[4,256,1024]{2,1,0:T(8,128)(2,1)}, u32[]{:S(2)}, u32[]{:S(2)}) collective-permute-start(bf16[4,256,1024]{2,1,0:T(8,128)(2,1)} %bitcast.94), channel_id=1, source_target_pairs={{0,1},{1,2},{2,3},{3,4},{4,5},{5,6},{6,7},{7,8},{8,9},{9,10},{10,1... | collective-permute-start | bytes 6291464 | tf_op jit(solution)/shard_map/ppermute | solution.py:18
  118.8 79.3 %copy-start.1 = (bf16[256,1024]{1,0:T(8,128)(2,1)S(1)}, bf16[256,1024]{1,0:T(8,128)(2,1)}, u32[]{:S(2)}) copy-start(bf16[256,1024]{1,0:T(8,128)(2,1)} %param.7) | copy-start | bytes 1572868
  204.8 428.0 %copy-start.5 = (f32[256]{0:T(256)}, f32[256]{0:T(256)S(1)}, u32[]{:S(2)}) copy-start(f32[256]{0:T(256)S(1)} %rsqrt.7) | copy-start | bytes 3076
  212.3 7.9 collective-permute-start.3
  213.6 9.8 collective-permute-start.2
  306.9 325.9 %copy-start.2 = (f32[32,32]{0,1:T(8,128)}, f32[32,32]{0,1:T(8,128)S(1)}, u32[]{:S(2)}) copy-start(f32[32,32]{0,1:T(8,128)S(1)} %psum.50) | copy-start | bytes 12292
  642.4 415.1 %copy-start.3 = (f32[32,32]{0,1:T(8,128)S(1)}, f32[32,32]{0,1:T(8,128)}, u32[]{:S(2)}) copy-start(f32[32,32]{0,1:T(8,128)} %copy-done.2) | copy-start | bytes 12292
  642.4 415.1 %copy-start.4 = (f32[1,32,32]{1,2,0:T(8,128)S(1)}, f32[1,32,32]{1,2,0:T(8,128)}, u32[]{:S(2)}) copy-start(f32[1,32,32]{1,2,0:T(8,128)} %get-tuple-element.12) | copy-start | bytes 12292
  642.4 6.8 collective-permute-start.5
  643.7 6.4 collective-permute-start.4
Sparse Core Ops, SparseCore 0:
  9.8 33.8 all-gather.4
